TPU v7x, 32 devices: a whole 2x2x4 slice. The times are simulated.
32 devices in a mesh: gx: 4 (over y, core), gy: 8 (over z, x).
Axes of the slice: x: 2, y: 2, z: 4, core: 2. Of those that a mesh axis runs over, the one named last changes fastest.
Arguments:
- flow_fields: float32 [6, 16, 256, 1024], P(None, None, 'gx', 'gy'), may hold values from -6 to 6
- cell_index: int32 [3, 32768], P(None, ('gx', 'gy')), may hold values from 0 to 127, as said below
- stencil_shift: int32 [3, 32768], P(None, ('gx', 'gy')), may hold values from -1 to 0
- fraction_in_cell: float32 [3, 32768], P(None, ('gx', 'gy')), may hold values from 0 to 1
- bubble_speed: float32 [3, 32768], P(None, ('gx', 'gy')), may hold values from -6 to 6
- history: float32 [3, 256, 32768], P(None, None, ('gx', 'gy')), may hold values from -4 to 4
- live_count: int32 [32], P(('gx', 'gy')), may hold values from 512 to 1024, as said below
- mig_slots: int32 [32, 8, 16], P(('gx', 'gy')), may hold values from 0 to 1023, as said below
- mig_count: int32 [32, 8], P(('gx', 'gy')), may hold values from 0 to 16, as said below
Outputs:
- new_speed: float32 [3, 32768], P(None, ('gx', 'gy'))
- new_position: float32 [3, 32768], P(None, ('gx', 'gy'))
- new_history: float32 [3, 256, 32768], P(None, None, ('gx', 'gy'))
- arrived_state: float32 [8, 6, 512], P(None, None, ('gx', 'gy'))
- arrived_history: float32 [8, 3, 256, 512], P(None, None, None, ('gx', 'gy'))
Inputs may be any that keep to these rules, and one draw needn't show every extreme that they name: `cell_index`: each component lies in its tile: x below 64, y below 128, z below 16. `live_count`: at least half of 1024 and at least 128; some tile is full. `mig_slots`: the used entries of a tile's 8 lists are distinct live slots of that tile; entries past the count are slots too and are ignored. `mig_count`: some list is full in every draw.
All inputs are finite; a program needn't handle non-finite values.
Results may differ from a plain program's by a relative error of at most 0.0003.
Values sent between devices are 32-bit elements; how exact they have to be, the bound alone decides.
A program may use at most 192 MiB of HBM per device.

v0:
```python
import functools

import jax
import jax.numpy as jnp
from jax import lax
from jax.experimental import pallas as pl
from jax.experimental.pallas import tpu as pltpu
from jax.sharding import PartitionSpec as P

neighbours = ((-1, -1), (-1, 0), (-1, 1), (0, -1), (0, 1), (1, -1), (1, 0), (1, 1))
step_dt = 0.1
relax_tau = 0.5
basset_coef = 0.3
MESH = pl.DeviceIdType.MESH
F32 = jnp.float32
BF16 = jnp.bfloat16


def basis_rows(s):
    return (
        -s * (s - 1.0) * (s - 2.0) / 6.0,
        (s + 1.0) * (s - 1.0) * (s - 2.0) / 2.0,
        -(s + 1.0) * s * (s - 2.0) / 2.0,
        (s + 1.0) * s * (s - 1.0) / 6.0,
    )


def pick_weight(d, w):
    out = jnp.where(d == 0, w[0], 0.0)
    for p in range(1, 4):
        out = jnp.where(d == p, w[p], out)
    return out


def split(v):
    hi = v.astype(BF16)
    return hi, (v - hi.astype(F32)).astype(BF16)


def iota(shape, dim):
    return lax.broadcasted_iota(jnp.int32, shape, dim)


def contract_lanes(a, b):
    return lax.dot_general(a, b, (((1,), (1,)), ((), ())), preferred_element_type=F32)


def main_kernel(
    sizes,
    live, counts, slots, cell, shift, frac, speed, flow, hist,
    res, rec_hist, rec_state, moved,
    i_cell, i_shift, i_frac, i_speed, i_slots, i_counts,
    f_buf, h_buf, a3, w_lv, w3, sx, rx, ty, sy, ry, fl, sel, mslot, hhi, hlo, tail_s, s_hist, s_state,
    sem_i, sem_f, sem_h, sem_xs, sem_xr, sem_ys, sem_yr, sem_rs, sem_rr, sem_ss, sem_sr,
):
    nx, ny, nz, nb, cap, steps, chunk, gx_n, gy_n = sizes
    zx = nz * nx
    xh = 4 * nz
    half = 2 * nz
    k3 = 3 * zx
    m = 6 * ny
    gx = lax.axis_index("gx")
    gy = lax.axis_index("gy")
    wrap_x = lambda i: lax.rem(gx + i + gx_n, gx_n)
    wrap_y = lambda i: lax.rem(gy + i + gy_n, gy_n)

    def f_copy(c):
        return pltpu.make_async_copy(flow.at[c], f_buf.at[c], sem_f.at[c])

    def h_copy(c):
        return pltpu.make_async_copy(hist.at[c], h_buf.at[c], sem_h.at[c])

    small = [
        pltpu.make_async_copy(a, b, sem_i.at[i])
        for i, (a, b) in enumerate(
            (
                (cell, i_cell), (shift, i_shift), (frac, i_frac), (speed, i_speed),
                (slots, i_slots), (counts, i_counts),
            )
        )
    ]
    for c in range(6):
        f_copy(c).start()
    for cp in small:
        cp.start()
    for c in range(3):
        h_copy(c).start()

    barrier = pltpu.get_barrier_semaphore()
    for dx, dy in neighbours:
        pl.semaphore_signal(barrier, inc=1, device_id=(wrap_x(dx), wrap_y(dy)), device_id_type=MESH)
    sy[...] = jnp.zeros_like(sy)

    def pack_x(c, _):
        f_copy(c).wait()
        for z in range(nz):
            sx[0, c, 2 * z : 2 * z + 2, :] = f_buf[c, z, 0:2, :]
            sx[1, c, 2 * z : 2 * z + 2, :] = f_buf[c, z, nx - 2 : nx, :]
        return 0

    lax.fori_loop(0, 6, pack_x, 0)
    pl.semaphore_wait(barrier, 8)
    x_copies = [
        pltpu.make_async_remote_copy(
            src_ref=sx.at[side], dst_ref=rx.at[1 - side], send_sem=sem_xs.at[side],
            recv_sem=sem_xr.at[1 - side], device_id=(wrap_x(2 * side - 1), gy), device_id_type=MESH,
        )
        for side in range(2)
    ]
    for cp in x_copies:
        cp.start()

    def weights(cells, shifts, fracs):
        base = cells + shifts
        w = basis_rows(fracs - shifts.astype(F32))

        def along(pos, dim):
            d = pos - base[dim : dim + 1] + 1
            if dim == 2:
                d = jnp.where(d < 0, d + nz, jnp.where(d >= nz, d - nz, d))
            return pick_weight(d, [v[dim : dim + 1] for v in w])

        return along

    def build_w(w3, width, along):
        wx = along(iota((nx, width), 0), 0)
        wz = along(iota((nz, width), 0), 2)
        for z in range(nz):
            hi, lo = split(wx * wz[z : z + 1])
            w3[z * nx : (z + 1) * nx] = hi
            w3[zx + z * nx : zx + (z + 1) * nx] = hi
            w3[2 * zx + z * nx : 2 * zx + (z + 1) * nx] = lo
        r = iota((xh, width), 0)
        far = r >= half
        q = jnp.where(far, r - half, r)
        hi, lo = split(along(jnp.where(far, nx, -2) + (q & 1), 0) * along(q >> 1, 2))
        w3[k3 : k3 + xh] = hi
        w3[k3 + xh : k3 + 2 * xh] = hi
        w3[k3 + 2 * xh : k3 + 3 * xh] = lo
        w3[k3 + 3 * xh : k3 + 4 * xh] = jnp.zeros_like(lo)

    def interpolate(w3, width, along):
        p = jnp.dot(a3[...], w3[...], preferred_element_type=F32)
        wy = along(iota((ny, width), 0), 1)
        inner = jnp.sum(p[0:m].reshape(6, ny, width) * wy[None], axis=1)
        wyh = [along(y, 1) for y in (-2, -1, ny, ny + 1)]
        outer = []
        for c in range(6):
            at = m + 2 * c
            extra = p[at : at + 1] * wyh[0] + p[at + 1 : at + 2] * wyh[1]
            at += 16
            outer.append(extra + p[at : at + 1] * wyh[2] + p[at + 1 : at + 2] * wyh[3])
        return inner + jnp.concatenate(outer, axis=0)

    def advance(fluid, v0, fracs, tail):
        fluid_u = fluid[0:3]
        fluid_a = fluid[3:6]

        def rate(v):
            return 3.0 * fluid_a + (fluid_u - v) / relax_tau + basset_coef * (fluid_u - v + tail)

        v1 = v0 + step_dt * rate(v0)
        v2 = 0.75 * v0 + 0.25 * (v1 + step_dt * rate(v1))
        vn = v0 / 3.0 + 2.0 / 3.0 * (v2 + step_dt * rate(v2))
        posn = fracs + step_dt * (v0 / 6.0 + v1 / 6.0 + 2.0 * v2 / 3.0)
        return vn, posn, fluid_u - vn

    for c in range(6):
        t = jnp.transpose(f_buf[c].reshape(zx, ny))
        hi, lo = split(t)
        rows = slice(c * ny, (c + 1) * ny)
        a3[rows, 0:zx] = hi
        a3[rows, zx : 2 * zx] = lo
        a3[rows, 2 * zx : 3 * zx] = hi
        ty[c, 0:2, 0:zx] = t[0:2]
        ty[c, 2:4, 0:zx] = t[ny - 2 : ny]

    for cp in x_copies:
        cp.wait()

    for c in range(6):
        block = jnp.concatenate([rx[0, c], rx[1, c], jnp.zeros((ny - xh, ny), F32)], axis=0)
        t = jnp.transpose(block)
        ty[c, 0:2, zx : zx + ny] = t[0:2]
        ty[c, 2:4, zx : zx + ny] = t[ny - 2 : ny]
        hi = t.astype(BF16).astype(F32)
        lo = t - hi
        rows = slice(c * ny, (c + 1) * ny)
        a3[rows, k3 : k3 + ny] = (hi + pltpu.roll(lo, xh, 1)).astype(BF16)
        a3[rows, k3 + ny : k3 + 2 * ny] = hi.astype(BF16)
    for c in range(6):
        sy[0, 2 * c : 2 * c + 2, :] = ty[c, 0:2, :]
        sy[1, 2 * c : 2 * c + 2, :] = ty[c, 2:4, :]
    y_copies = [
        pltpu.make_async_remote_copy(
            src_ref=sy.at[side], dst_ref=ry.at[1 - side], send_sem=sem_ys.at[side],
            recv_sem=sem_yr.at[1 - side], device_id=(gx, wrap_y(2 * side - 1)), device_id_type=MESH,
        )
        for side in range(2)
    ]
    for cp in y_copies:
        cp.start()

    for cp in small:
        cp.wait()

    mslot[...] = jnp.zeros_like(mslot)
    mslot[0:8, 0:cap] = i_slots[0].astype(F32)
    cols_t = jnp.transpose(mslot[...])
    for d in range(8):
        col = cols_t[0:cap, d : d + 1]
        col = jnp.where(iota((cap, 1), 0) < i_counts[0, d], col, -1.0).astype(jnp.int32)
        sel[d * cap : (d + 1) * cap, :] = (iota((cap, nb), 1) == col).astype(F32).astype(BF16)
    karg = iota((steps, 128), 0).astype(F32) + 1.0
    quad = (jnp.sqrt(karg + 1.0) - jnp.sqrt(karg))[:, 0:1]

    alive = iota((1, nb), 1) < live[0]
    for c in range(3):
        h_copy(c).wait()
    for c in range(3):
        h = h_buf[c]
        tail_s[c] = jnp.sum(h * quad, axis=0, keepdims=True)
        hi, lo = split(h)
        hhi[c] = hi
        hlo[c] = lo
        picked = contract_lanes(sel[...], hhi[c]) + contract_lanes(sel[...], hlo[c])
        picked = pltpu.roll(picked, 1, 1)
        s_hist[:, :, c * steps : (c + 1) * steps] = picked.reshape(8, cap, steps)
        moved[c] = jnp.where(alive, pltpu.roll(h, 1, 0), 0.0)
    r_copies = [
        pltpu.make_async_remote_copy(
            src_ref=s_hist.at[d], dst_ref=rec_hist.at[d], send_sem=sem_rs.at[d],
            recv_sem=sem_rr.at[d], device_id=(wrap_x(dx), wrap_y(dy)), device_id_type=MESH,
        )
        for d, (dx, dy) in enumerate(neighbours)
    ]
    for cp in r_copies:
        cp.start()

    leaving = 8 * cap
    tail = jnp.concatenate([tail_s[c] for c in range(3)], axis=0)
    own = jnp.concatenate(
        [
            i_cell[...].astype(F32), i_shift[...].astype(F32), i_frac[...], i_speed[...], tail,
            jnp.ones((1, nb), F32),
        ],
        axis=0,
    )
    hi, lo = split(own)
    own = contract_lanes(hi, sel[...]) + contract_lanes(lo, sel[...])
    lv_along = weights(own[0:3].astype(jnp.int32), own[3:6].astype(jnp.int32), own[6:9])
    build_w(w_lv, leaving, lv_along)

    for cp in y_copies:
        cp.wait()
    for side in range(2):
        rows = slice(m + 16 * side, m + 16 * side + 16)
        v = ry[side]
        hi, lo = split(v[:, 0:zx])
        a3[rows, 0:zx] = hi
        a3[rows, zx : 2 * zx] = lo
        a3[rows, 2 * zx : 3 * zx] = hi
        t = v[:, zx : zx + ny]
        thi = t.astype(BF16).astype(F32)
        a3[rows, k3 : k3 + ny] = (thi + pltpu.roll(t - thi, xh, 1)).astype(BF16)
        a3[rows, k3 + ny : k3 + 2 * ny] = thi.astype(BF16)

    chunks = nb // chunk
    spans = [slice(j * chunk, (j + 1) * chunk) for j in range(chunks)]
    along = [weights(i_cell[:, g], i_shift[:, g], i_frac[:, g]) for g in spans]
    build_w(w3.at[0], chunk, along[0])
    lv = advance(interpolate(w_lv, leaving, lv_along), own[9:12], own[6:9], own[12:15])
    used = own[15:16] > 0.5
    mslot[...] = jnp.zeros_like(mslot)
    for i, v in enumerate(lv):
        mslot[3 * i : 3 * i + 3, :] = jnp.where(used, v, 0.0)
    s_state[...] = jnp.transpose(mslot[...]).reshape(8, cap, 128)
    s_copies = [
        pltpu.make_async_remote_copy(
            src_ref=s_state.at[d], dst_ref=rec_state.at[d], send_sem=sem_ss.at[d],
            recv_sem=sem_sr.at[d], device_id=(wrap_x(dx), wrap_y(dy)), device_id_type=MESH,
        )
        for d, (dx, dy) in enumerate(neighbours)
    ]
    for cp in s_copies:
        cp.start()

    for j in range(chunks):
        if j + 1 < chunks:
            build_w(w3.at[j + 1], chunk, along[j + 1])
        fl[0:6, spans[j]] = interpolate(w3.at[j], chunk, along[j])

    keep = iota((3, nb), 1) < live[0]
    for i, v in enumerate(advance(fl[0:6, :], i_speed[...], i_frac[...], tail)):
        res[3 * i : 3 * i + 3, :] = jnp.where(keep, v, 0.0)
    res[9:16, :] = jnp.zeros((7, nb), F32)

    for c in range(3):
        moved[c, 0:1, :] = res[6 + c : 7 + c, :]
    for cp in r_copies + s_copies:
        cp.wait()


def finish_kernel(
    cap, steps,
    res, rec_hist, rec_state, moved,
    vn, posn, out_hist, arr_state, arr_hist,
    b_vn, b_posn, b_state, b_hist, sems,
):
    copies = [pltpu.make_async_copy(moved, out_hist, sems.at[0])]
    copies[0].start()

    def send(src, dst):
        cp = pltpu.make_async_copy(src, dst, sems.at[len(copies)])
        cp.start()
        copies.append(cp)

    b_vn[...] = res[0:3, :]
    send(b_vn, vn)
    b_posn[...] = res[3:6, :]
    send(b_posn, posn)
    t = jnp.transpose(rec_state[...].reshape(8 * cap, 128))
    for d in range(8):
        b_state[:, d, :] = t[0:6, d * cap : (d + 1) * cap]
    send(b_state, arr_state)
    first = iota((cap, steps), 1) == 0
    for d in range(8):
        for c in range(3):
            col = rec_state[d, :, 6 + c : 7 + c]
            b_hist[d, c] = jnp.where(first, col, rec_hist[d, :, c * steps : (c + 1) * steps])
    send(b_hist, arr_hist)
    for cp in copies:
        cp.wait()


def on_device(flow, cell, shift, frac, speed, hist, live, slots, counts):
    _, nz, nx, ny = flow.shape
    nb = speed.shape[1]
    steps = hist.shape[1]
    cap = slots.shape[2]
    zx = nz * nx
    k3 = 3 * zx + 4 * 4 * nz
    chunk = 512
    sizes = (nx, ny, nz, nb, cap, steps, chunk, lax.axis_size("gx"), lax.axis_size("gy"))
    vmem = pl.BlockSpec(memory_space=pltpu.VMEM)
    hbm = pl.BlockSpec(memory_space=pltpu.HBM)
    dma = pltpu.SemaphoreType.DMA
    I32 = jnp.int32
    inputs = (counts, slots, cell, shift, frac, speed, flow, hist)
    gathered = pl.pallas_call(
        functools.partial(main_kernel, sizes),
        out_shape=(
            jax.ShapeDtypeStruct((16, nb), F32),
            jax.ShapeDtypeStruct((8, cap, 3 * steps), F32),
            jax.ShapeDtypeStruct((8, cap, 128), F32),
            jax.ShapeDtypeStruct((3, steps, nb), F32),
        ),
        in_specs=[pl.BlockSpec(memory_space=pltpu.SMEM)] + [hbm] * 8,
        out_specs=[vmem] * 4,
        scratch_shapes=[
            pltpu.VMEM((3, nb), I32),
            pltpu.VMEM((3, nb), I32),
            pltpu.VMEM((3, nb), F32),
            pltpu.VMEM((3, nb), F32),
            pltpu.VMEM((1, 8, cap), I32),
            pltpu.SMEM((1, 8), I32),
            pltpu.VMEM((6, nz, nx, ny), F32),
            pltpu.VMEM((3, steps, nb), F32),
            pltpu.VMEM((6 * ny + 32, k3), BF16),
            pltpu.VMEM((k3, 8 * cap), BF16),
            pltpu.VMEM((nb // chunk, k3, chunk), BF16),
            pltpu.VMEM((2, 6, 2 * nz, ny), F32),
            pltpu.VMEM((2, 6, 2 * nz, ny), F32),
            pltpu.VMEM((6, 8, zx + ny), F32),
            pltpu.VMEM((2, 16, zx + ny), F32),
            pltpu.VMEM((2, 16, zx + ny), F32),
            pltpu.VMEM((8, nb), F32),
            pltpu.VMEM((8 * cap, nb), BF16),
            pltpu.VMEM((128, 128), F32),
            pltpu.VMEM((3, steps, nb), BF16),
            pltpu.VMEM((3, steps, nb), BF16),
            pltpu.VMEM((3, 1, nb), F32),
            pltpu.VMEM((8, cap, 3 * steps), F32),
            pltpu.VMEM((8, cap, 128), F32),
            dma((6,)), dma((6,)), dma((3,)), dma((2,)), dma((2,)), dma((2,)), dma((2,)),
            dma((8,)), dma((8,)), dma((8,)), dma((8,)),
        ],
        compiler_params=pltpu.CompilerParams(
            collective_id=0, has_side_effects=True, vmem_limit_bytes=44 * 2**20
        ),
        name="interpolate_and_migrate",
    )(live, *(pltpu.with_memory_space_constraint(v, pltpu.HBM) for v in inputs))

    vn, posn, out_hist, arr_state, arr_hist = pl.pallas_call(
        functools.partial(finish_kernel, cap, steps),
        out_shape=(
            jax.ShapeDtypeStruct((3, nb), F32),
            jax.ShapeDtypeStruct((3, nb), F32),
            jax.ShapeDtypeStruct((3, steps, nb), F32),
            jax.ShapeDtypeStruct((6, 8, cap), F32),
            jax.ShapeDtypeStruct((8, 3, cap, steps), F32),
        ),
        in_specs=[vmem] * 4,
        out_specs=[hbm] * 5,
        scratch_shapes=[
            pltpu.VMEM((3, nb), F32),
            pltpu.VMEM((3, nb), F32),
            pltpu.VMEM((6, 8, cap), F32),
            pltpu.VMEM((8, 3, cap, steps), F32),
            dma((5,)),
        ],
        compiler_params=pltpu.CompilerParams(vmem_limit_bytes=32 * 2**20),
        name="write_results",
    )(*gathered)
    return (
        vn,
        posn,
        out_hist,
        jnp.transpose(arr_state, (1, 0, 2)),
        jnp.transpose(arr_hist, (0, 1, 3, 2)),
    )


def solution(mesh):
    placed = (
        P(None, None, "gx", "gy"),
        P(None, ("gx", "gy")),
        P(None, ("gx", "gy")),
        P(None, ("gx", "gy")),
        P(None, ("gx", "gy")),
        P(None, None, ("gx", "gy")),
        P(("gx", "gy")),
        P(("gx", "gy"), None, None),
        P(("gx", "gy"), None),
    )
    return jax.shard_map(
        on_device,
        mesh=mesh,
        in_specs=placed,
        out_specs=(
            P(None, ("gx", "gy")),
            P(None, ("gx", "gy")),
            P(None, None, ("gx", "gy")),
            P(None, None, ("gx", "gy")),
            P(None, None, None, ("gx", "gy")),
        ),
        check_vma=False,
    )
```

profile of v0, /device:TPU:0, one launch (start us, length us, event | category | flops | bytes accessed | tf_op | source)
XLA Modules:
  0.0 28.3 jit_solution(4623392900927786571)
XLA Ops:
  1.3 25.0 %interpolate_and_migrate.1 = (f32[16,1024]{1,0:T(8,128)S(1)}, f32[8,16,768]{2,1,0:T(8,128)S(1)}, f32[8,16,128]{2,1,0:T(8,128)S(1)}, f32[3,256,1024]{2,1,0:T(8,128)S(1)}) custom-call(s32[1]{0:T(128)S(6)} %copy.14.live, s32[1,8]{1,0:T(1,128)} %counts.1, s32[1,8,16]{2,1,0:T(8,128)} %slots.1, s32[3,1024]{1,0:T(4,128)} %cell.1, s32[3,1024]{1,0:T(4,128)} %shift.1, ...), custom_call_target="tpu_custom_call" | custom-call | tf_op jit(solution)/shard_map/interpolate_and_migrate/pallas_call | solution.py:350
  26.3 2.0 %write_results.1 = (f32[3,1024]{1,0:T(4,128)}, f32[3,1024]{1,0:T(4,128)}, f32[3,256,1024]{2,1,0:T(8,128)}, f32[6,8,16]{2,1,0:T(8,128)}, f32[8,3,16,256]{3,2,1,0:T(8,128)}) custom-call(f32[16,1024]{1,0:T(8,128)S(1)} %get-tuple-element.14.res, f32[8,16,768]{2,1,0:T(8,128)S(1)} %get-tuple-element.15.rec_hist, f32[8,16,128]{2,1,0:T(8,128)S(1)} %get-tuple-element.16.rec_state, ...), custom_call_target="tpu_custom_call" | custom-call | tf_op jit(solution)/shard_map/write_results/pallas_call | solution.py:394
where the time goes:
time: 28.4 us; the launch traced here: 28.3 us
  Pallas kernels  27 us (95%)
  between operations  1.29 us (5%)
    pallas_call x1, Pallas kernels, on_device(): pl.pallas_call(functools.partial(main_kernel, sizes), out_shape=(jax.Shap...  25 us
    pallas_call x1, Pallas kernels, on_device(): pl.pallas_call(functools.partial(finish_kernel, cap, steps), out_shape=(j...  1.96 us

commit v1 on v0

--- a/solution.py
+++ b/solution.py
@@ -50,8 +50,8 @@
     live, counts, slots, cell, shift, frac, speed, flow, hist,
     res, rec_hist, rec_state, moved,
     i_cell, i_shift, i_frac, i_speed, i_slots, i_counts,
-    f_buf, h_buf, a3, w_lv, w3, sx, rx, ty, sy, ry, fl, sel, mslot, hhi, hlo, tail_s, s_hist, s_state,
-    sem_i, sem_f, sem_h, sem_xs, sem_xr, sem_ys, sem_yr, sem_rs, sem_rr, sem_ss, sem_sr,
+    f_buf, h_buf, a3, w_lv, w3, sx, rx, sy, ry, sc, rc, ys, fl, sel, mslot, hhi, hlo, tail_s, s_hist, s_state,
+    sem_i, sem_f, sem_h, sem_xs, sem_xr, sem_ys, sem_yr, sem_cs, sem_cr, sem_rs, sem_rr, sem_ss, sem_sr,
 ):
     nx, ny, nz, nb, cap, steps, chunk, gx_n, gy_n = sizes
     zx = nz * nx
@@ -89,7 +89,13 @@
     barrier = pltpu.get_barrier_semaphore()
     for dx, dy in neighbours:
         pl.semaphore_signal(barrier, inc=1, device_id=(wrap_x(dx), wrap_y(dy)), device_id_type=MESH)
-    sy[...] = jnp.zeros_like(sy)
+    ys[...] = jnp.zeros_like(ys)
+
+    def y_copy(src, dst, sem_s, sem_r, side):
+        return pltpu.make_async_remote_copy(
+            src_ref=src.at[side], dst_ref=dst.at[1 - side], send_sem=sem_s.at[side],
+            recv_sem=sem_r.at[1 - side], device_id=(gx, wrap_y(2 * side - 1)), device_id_type=MESH,
+        )
 
     def pack_x(c, _):
         f_copy(c).wait()
@@ -139,18 +145,26 @@
         w3[k3 + 2 * xh : k3 + 3 * xh] = lo
         w3[k3 + 3 * xh : k3 + 4 * xh] = jnp.zeros_like(lo)
 
-    def interpolate(w3, width, along):
-        p = jnp.dot(a3[...], w3[...], preferred_element_type=F32)
+    def product(lo_row, hi_row, w3):
+        return jnp.dot(a3[lo_row:hi_row, :], w3[...], preferred_element_type=F32)
+
+    def inner_sum(p, width, along):
         wy = along(iota((ny, width), 0), 1)
-        inner = jnp.sum(p[0:m].reshape(6, ny, width) * wy[None], axis=1)
+        return jnp.sum(p.reshape(6, ny, width) * wy[None], axis=1)
+
+    def outer_sum(p, along):
         wyh = [along(y, 1) for y in (-2, -1, ny, ny + 1)]
         outer = []
         for c in range(6):
-            at = m + 2 * c
+            at = 2 * c
             extra = p[at : at + 1] * wyh[0] + p[at + 1 : at + 2] * wyh[1]
             at += 16
             outer.append(extra + p[at : at + 1] * wyh[2] + p[at + 1 : at + 2] * wyh[3])
-        return inner + jnp.concatenate(outer, axis=0)
+        return jnp.concatenate(outer, axis=0)
+
+    def interpolate(w3, width, along):
+        p = product(0, m + 32, w3)
+        return inner_sum(p[0:m], width, along) + outer_sum(p[m:], along)
 
     def advance(fluid, v0, fracs, tail):
         fluid_u = fluid[0:3]
@@ -172,8 +186,12 @@
         a3[rows, 0:zx] = hi
         a3[rows, zx : 2 * zx] = lo
         a3[rows, 2 * zx : 3 * zx] = hi
-        ty[c, 0:2, 0:zx] = t[0:2]
-        ty[c, 2:4, 0:zx] = t[ny - 2 : ny]
+        pair = slice(2 * (c % 2), 2 * (c % 2) + 2)
+        sy[0, c // 2, pair, :] = t[0:2]
+        sy[1, c // 2, pair, :] = t[ny - 2 : ny]
+    y_copies = [y_copy(sy, ry, sem_ys, sem_yr, side) for side in range(2)]
+    for cp in y_copies:
+        cp.start()
 
     for cp in x_copies:
         cp.wait()
@@ -181,24 +199,16 @@
     for c in range(6):
         block = jnp.concatenate([rx[0, c], rx[1, c], jnp.zeros((ny - xh, ny), F32)], axis=0)
         t = jnp.transpose(block)
-        ty[c, 0:2, zx : zx + ny] = t[0:2]
-        ty[c, 2:4, zx : zx + ny] = t[ny - 2 : ny]
+        pair = slice(2 * (c % 2), 2 * (c % 2) + 2)
+        sc[0, c // 2, pair, :] = t[0:2]
+        sc[1, c // 2, pair, :] = t[ny - 2 : ny]
         hi = t.astype(BF16).astype(F32)
         lo = t - hi
         rows = slice(c * ny, (c + 1) * ny)
         a3[rows, k3 : k3 + ny] = (hi + pltpu.roll(lo, xh, 1)).astype(BF16)
         a3[rows, k3 + ny : k3 + 2 * ny] = hi.astype(BF16)
-    for c in range(6):
-        sy[0, 2 * c : 2 * c + 2, :] = ty[c, 0:2, :]
-        sy[1, 2 * c : 2 * c + 2, :] = ty[c, 2:4, :]
-    y_copies = [
-        pltpu.make_async_remote_copy(
-            src_ref=sy.at[side], dst_ref=ry.at[1 - side], send_sem=sem_ys.at[side],
-            recv_sem=sem_yr.at[1 - side], device_id=(gx, wrap_y(2 * side - 1)), device_id_type=MESH,
-        )
-        for side in range(2)
-    ]
-    for cp in y_copies:
+    c_copies = [y_copy(sc, rc, sem_cs, sem_cr, side) for side in range(2)]
+    for cp in c_copies:
         cp.start()
 
     for cp in small:
@@ -251,11 +261,22 @@
     lv_along = weights(own[0:3].astype(jnp.int32), own[3:6].astype(jnp.int32), own[6:9])
     build_w(w_lv, leaving, lv_along)
 
-    for cp in y_copies:
+    chunks = nb // chunk
+    spans = [slice(j * chunk, (j + 1) * chunk) for j in range(chunks)]
+    along = [weights(i_cell[:, g], i_shift[:, g], i_frac[:, g]) for g in spans]
+    build_w(w3.at[0], chunk, along[0])
+    for j in range(1, chunks):
+        build_w(w3.at[j], chunk, along[j])
+    fl[0:6, spans[0]] = inner_sum(product(0, m, w3.at[0]), chunk, along[0])
+
+    for cp in y_copies + c_copies:
         cp.wait()
     for side in range(2):
         rows = slice(m + 16 * side, m + 16 * side + 16)
-        v = ry[side]
+        for g in range(3):
+            ys[side, 4 * g : 4 * g + 4, 0:zx] = ry[side, g]
+            ys[side, 4 * g : 4 * g + 4, zx : zx + ny] = rc[side, g]
+        v = ys[side]
         hi, lo = split(v[:, 0:zx])
         a3[rows, 0:zx] = hi
         a3[rows, zx : 2 * zx] = lo
@@ -265,10 +286,6 @@
         a3[rows, k3 : k3 + ny] = (thi + pltpu.roll(t - thi, xh, 1)).astype(BF16)
         a3[rows, k3 + ny : k3 + 2 * ny] = thi.astype(BF16)
 
-    chunks = nb // chunk
-    spans = [slice(j * chunk, (j + 1) * chunk) for j in range(chunks)]
-    along = [weights(i_cell[:, g], i_shift[:, g], i_frac[:, g]) for g in spans]
-    build_w(w3.at[0], chunk, along[0])
     lv = advance(interpolate(w_lv, leaving, lv_along), own[9:12], own[6:9], own[12:15])
     used = own[15:16] > 0.5
     mslot[...] = jnp.zeros_like(mslot)
@@ -285,9 +302,8 @@
     for cp in s_copies:
         cp.start()
 
-    for j in range(chunks):
-        if j + 1 < chunks:
-            build_w(w3.at[j + 1], chunk, along[j + 1])
+    fl[0:6, spans[0]] += outer_sum(product(m, m + 32, w3.at[0]), along[0])
+    for j in range(1, chunks):
         fl[0:6, spans[j]] = interpolate(w3.at[j], chunk, along[j])
 
     keep = iota((3, nb), 1) < live[0]
@@ -371,8 +387,10 @@
             pltpu.VMEM((nb // chunk, k3, chunk), BF16),
             pltpu.VMEM((2, 6, 2 * nz, ny), F32),
             pltpu.VMEM((2, 6, 2 * nz, ny), F32),
-            pltpu.VMEM((6, 8, zx + ny), F32),
-            pltpu.VMEM((2, 16, zx + ny), F32),
+            pltpu.VMEM((2, 3, 4, zx), F32),
+            pltpu.VMEM((2, 3, 4, zx), F32),
+            pltpu.VMEM((2, 3, 4, ny), F32),
+            pltpu.VMEM((2, 3, 4, ny), F32),
             pltpu.VMEM((2, 16, zx + ny), F32),
             pltpu.VMEM((8, nb), F32),
             pltpu.VMEM((8 * cap, nb), BF16),
@@ -383,6 +401,7 @@
             pltpu.VMEM((8, cap, 3 * steps), F32),
             pltpu.VMEM((8, cap, 128), F32),
             dma((6,)), dma((6,)), dma((3,)), dma((2,)), dma((2,)), dma((2,)), dma((2,)),
+            dma((2,)), dma((2,)),
             dma((8,)), dma((8,)), dma((8,)), dma((8,)),
         ],
         compiler_params=pltpu.CompilerParams(

time: 28.4 us -> 26.5 us (0.933)
  the two profiles are of different devices: /device:TPU:0 before, /device:TPU:1 now
where the time goes in v1:
time: 26.5 us; the launch traced here: 26.3 us
  Pallas kernels  25 us (94%)
  between operations  1.29 us (5%)
    pallas_call x1, Pallas kernels, on_device(): pl.pallas_call(functools.partial(main_kernel, sizes), out_shape=(jax.Shap...  23.1 us
    pallas_call x1, Pallas kernels, on_device(): pl.pallas_call(functools.partial(finish_kernel, cap, steps), out_shape=(j...  1.96 us

profile of v1, /device:TPU:1, one launch (start us, length us, event | category | flops | bytes accessed | tf_op | source)
XLA Modules:
  0.0 26.3 jit_solution(8417545521289353909)
XLA Ops:
  1.3 23.1 %interpolate_and_migrate.1 = (f32[16,1024]{1,0:T(8,128)S(1)}, f32[8,16,768]{2,1,0:T(8,128)S(1)}, f32[8,16,128]{2,1,0:T(8,128)S(1)}, f32[3,256,1024]{2,1,0:T(8,128)S(1)}) custom-call(s32[1]{0:T(128)S(6)} %copy.14.live, s32[1,8]{1,0:T(1,128)} %counts.1, s32[1,8,16]{2,1,0:T(8,128)} %slots.1, s32[3,1024]{1,0:T(4,128)} %cell.1, s32[3,1024]{1,0:T(4,128)} %shift.1, ...), custom_call_target="tpu_custom_call" | custom-call | tf_op jit(solution)/shard_map/interpolate_and_migrate/pallas_call | solution.py:366
  24.3 2.0 %write_results.1 = (f32[3,1024]{1,0:T(4,128)}, f32[3,1024]{1,0:T(4,128)}, f32[3,256,1024]{2,1,0:T(8,128)}, f32[6,8,16]{2,1,0:T(8,128)}, f32[8,3,16,256]{3,2,1,0:T(8,128)}) custom-call(f32[16,1024]{1,0:T(8,128)S(1)} %get-tuple-element.14.res, f32[8,16,768]{2,1,0:T(8,128)S(1)} %get-tuple-element.15.rec_hist, f32[8,16,128]{2,1,0:T(8,128)S(1)} %get-tuple-element.16.rec_state, ...), custom_call_target="tpu_custom_call" | custom-call | tf_op jit(solution)/shard_map/write_results/pallas_call | solution.py:413

commit v2 on v1

--- a/solution.py
+++ b/solution.py
@@ -105,17 +105,6 @@
         return 0
 
     lax.fori_loop(0, 6, pack_x, 0)
-    pl.semaphore_wait(barrier, 8)
-    x_copies = [
-        pltpu.make_async_remote_copy(
-            src_ref=sx.at[side], dst_ref=rx.at[1 - side], send_sem=sem_xs.at[side],
-            recv_sem=sem_xr.at[1 - side], device_id=(wrap_x(2 * side - 1), gy), device_id_type=MESH,
-        )
-        for side in range(2)
-    ]
-    for cp in x_copies:
-        cp.start()
-
     def weights(cells, shifts, fracs):
         base = cells + shifts
         w = basis_rows(fracs - shifts.astype(F32))
@@ -189,26 +178,19 @@
         pair = slice(2 * (c % 2), 2 * (c % 2) + 2)
         sy[0, c // 2, pair, :] = t[0:2]
         sy[1, c // 2, pair, :] = t[ny - 2 : ny]
+    pl.semaphore_wait(barrier, 8)
+    x_copies = [
+        pltpu.make_async_remote_copy(
+            src_ref=sx.at[side], dst_ref=rx.at[1 - side], send_sem=sem_xs.at[side],
+            recv_sem=sem_xr.at[1 - side], device_id=(wrap_x(2 * side - 1), gy), device_id_type=MESH,
+        )
+        for side in range(2)
+    ]
+    for cp in x_copies:
+        cp.start()
+
     y_copies = [y_copy(sy, ry, sem_ys, sem_yr, side) for side in range(2)]
     for cp in y_copies:
-        cp.start()
-
-    for cp in x_copies:
-        cp.wait()
-
-    for c in range(6):
-        block = jnp.concatenate([rx[0, c], rx[1, c], jnp.zeros((ny - xh, ny), F32)], axis=0)
-        t = jnp.transpose(block)
-        pair = slice(2 * (c % 2), 2 * (c % 2) + 2)
-        sc[0, c // 2, pair, :] = t[0:2]
-        sc[1, c // 2, pair, :] = t[ny - 2 : ny]
-        hi = t.astype(BF16).astype(F32)
-        lo = t - hi
-        rows = slice(c * ny, (c + 1) * ny)
-        a3[rows, k3 : k3 + ny] = (hi + pltpu.roll(lo, xh, 1)).astype(BF16)
-        a3[rows, k3 + ny : k3 + 2 * ny] = hi.astype(BF16)
-    c_copies = [y_copy(sc, rc, sem_cs, sem_cr, side) for side in range(2)]
-    for cp in c_copies:
         cp.start()
 
     for cp in small:
@@ -267,6 +249,24 @@
     build_w(w3.at[0], chunk, along[0])
     for j in range(1, chunks):
         build_w(w3.at[j], chunk, along[j])
+    for cp in x_copies:
+        cp.wait()
+
+    for c in range(6):
+        block = jnp.concatenate([rx[0, c], rx[1, c], jnp.zeros((ny - xh, ny), F32)], axis=0)
+        t = jnp.transpose(block)
+        pair = slice(2 * (c % 2), 2 * (c % 2) + 2)
+        sc[0, c // 2, pair, :] = t[0:2]
+        sc[1, c // 2, pair, :] = t[ny - 2 : ny]
+        hi = t.astype(BF16).astype(F32)
+        lo = t - hi
+        rows = slice(c * ny, (c + 1) * ny)
+        a3[rows, k3 : k3 + ny] = (hi + pltpu.roll(lo, xh, 1)).astype(BF16)
+        a3[rows, k3 + ny : k3 + 2 * ny] = hi.astype(BF16)
+    c_copies = [y_copy(sc, rc, sem_cs, sem_cr, side) for side in range(2)]
+    for cp in c_copies:
+        cp.start()
+
     fl[0:6, spans[0]] = inner_sum(product(0, m, w3.at[0]), chunk, along[0])
 
     for cp in y_copies + c_copies:

time: 26.5 us -> 28.3 us (1.068)
  Pallas kernels: 25 us -> 26.6 us
    pallas_call x1, Pallas kernels: 23.1 us -> 24.6 us  [on_device(): pl.pallas_call(functools.partial(main_kernel, sizes), out_shape=(jax.Shap...]
where the time goes in v2:
time: 28.3 us; the launch traced here: 27.9 us
  Pallas kernels  26.6 us (94%)
  between operations  1.29 us (5%)
    pallas_call x1, Pallas kernels, on_device(): pl.pallas_call(functools.partial(main_kernel, sizes), out_shape=(jax.Shap...  24.6 us
    pallas_call x1, Pallas kernels, on_device(): pl.pallas_call(functools.partial(finish_kernel, cap, steps), out_shape=(j...  1.96 us

profile of v2, /device:TPU:1, one launch (start us, length us, event | category | flops | bytes accessed | tf_op | source)
XLA Modules:
  0.0 27.9 jit_solution(5111562154596352386)
XLA Ops:
  1.3 24.6 %interpolate_and_migrate.1 = (f32[16,1024]{1,0:T(8,128)S(1)}, f32[8,16,768]{2,1,0:T(8,128)S(1)}, f32[8,16,128]{2,1,0:T(8,128)S(1)}, f32[3,256,1024]{2,1,0:T(8,128)S(1)}) custom-call(s32[1]{0:T(128)S(6)} %copy.14.live, s32[1,8]{1,0:T(1,128)} %counts.1, s32[1,8,16]{2,1,0:T(8,128)} %slots.1, s32[3,1024]{1,0:T(4,128)} %cell.1, s32[3,1024]{1,0:T(4,128)} %shift.1, ...), custom_call_target="tpu_custom_call" | custom-call | tf_op jit(solution)/shard_map/interpolate_and_migrate/pallas_call | solution.py:366
  25.9 2.0 %write_results.1 = (f32[3,1024]{1,0:T(4,128)}, f32[3,1024]{1,0:T(4,128)}, f32[3,256,1024]{2,1,0:T(8,128)}, f32[6,8,16]{2,1,0:T(8,128)}, f32[8,3,16,256]{3,2,1,0:T(8,128)}) custom-call(f32[16,1024]{1,0:T(8,128)S(1)} %get-tuple-element.14.res, f32[8,16,768]{2,1,0:T(8,128)S(1)} %get-tuple-element.15.rec_hist, f32[8,16,128]{2,1,0:T(8,128)S(1)} %get-tuple-element.16.rec_state, ...), custom_call_target="tpu_custom_call" | custom-call | tf_op jit(solution)/shard_map/write_results/pallas_call | solution.py:413

commit v3 on v1

--- a/solution.py
+++ b/solution.py
@@ -193,6 +193,32 @@
     for cp in y_copies:
         cp.start()
 
+    for cp in small:
+        cp.wait()
+
+    mslot[...] = jnp.zeros_like(mslot)
+    mslot[0:8, 0:cap] = i_slots[0].astype(F32)
+    cols_t = jnp.transpose(mslot[...])
+    for d in range(8):
+        col = cols_t[0:cap, d : d + 1]
+        col = jnp.where(iota((cap, 1), 0) < i_counts[0, d], col, -1.0).astype(jnp.int32)
+        sel[d * cap : (d + 1) * cap, :] = (iota((cap, nb), 1) == col).astype(F32).astype(BF16)
+    karg = iota((steps, 128), 0).astype(F32) + 1.0
+    quad = (jnp.sqrt(karg + 1.0) - jnp.sqrt(karg))[:, 0:1]
+
+    alive = iota((1, nb), 1) < live[0]
+    for c in range(3):
+        h_copy(c).wait()
+    for c in range(3):
+        h = h_buf[c]
+        tail_s[c] = jnp.sum(h * quad, axis=0, keepdims=True)
+        hi, lo = split(h)
+        hhi[c] = hi
+        hlo[c] = lo
+        picked = contract_lanes(sel[...], hhi[c]) + contract_lanes(sel[...], hlo[c])
+        picked = pltpu.roll(picked, 1, 1)
+        s_hist[:, :, c * steps : (c + 1) * steps] = picked.reshape(8, cap, steps)
+        moved[c] = jnp.where(alive, pltpu.roll(h, 1, 0), 0.0)
     for cp in x_copies:
         cp.wait()
 
@@ -211,32 +237,6 @@
     for cp in c_copies:
         cp.start()
 
-    for cp in small:
-        cp.wait()
-
-    mslot[...] = jnp.zeros_like(mslot)
-    mslot[0:8, 0:cap] = i_slots[0].astype(F32)
-    cols_t = jnp.transpose(mslot[...])
-    for d in range(8):
-        col = cols_t[0:cap, d : d + 1]
-        col = jnp.where(iota((cap, 1), 0) < i_counts[0, d], col, -1.0).astype(jnp.int32)
-        sel[d * cap : (d + 1) * cap, :] = (iota((cap, nb), 1) == col).astype(F32).astype(BF16)
-    karg = iota((steps, 128), 0).astype(F32) + 1.0
-    quad = (jnp.sqrt(karg + 1.0) - jnp.sqrt(karg))[:, 0:1]
-
-    alive = iota((1, nb), 1) < live[0]
-    for c in range(3):
-        h_copy(c).wait()
-    for c in range(3):
-        h = h_buf[c]
-        tail_s[c] = jnp.sum(h * quad, axis=0, keepdims=True)
-        hi, lo = split(h)
-        hhi[c] = hi
-        hlo[c] = lo
-        picked = contract_lanes(sel[...], hhi[c]) + contract_lanes(sel[...], hlo[c])
-        picked = pltpu.roll(picked, 1, 1)
-        s_hist[:, :, c * steps : (c + 1) * steps] = picked.reshape(8, cap, steps)
-        moved[c] = jnp.where(alive, pltpu.roll(h, 1, 0), 0.0)
     r_copies = [
         pltpu.make_async_remote_copy(
             src_ref=s_hist.at[d], dst_ref=rec_hist.at[d], send_sem=sem_rs.at[d],

time: 26.5 us -> 25.6 us (0.966)
  Pallas kernels: 25 us -> 24.1 us
    pallas_call x1, Pallas kernels: 23.1 us -> 22.1 us  [on_device(): pl.pallas_call(functools.partial(main_kernel, sizes), out_shape=(jax.Shap...]
where the time goes in v3:
time: 25.6 us; the launch traced here: 25.4 us
  Pallas kernels  24.1 us (94%)
  between operations  1.29 us (5%)
    pallas_call x1, Pallas kernels, on_device(): pl.pallas_call(functools.partial(main_kernel, sizes), out_shape=(jax.Shap...  22.1 us
    pallas_call x1, Pallas kernels, on_device(): pl.pallas_call(functools.partial(finish_kernel, cap, steps), out_shape=(j...  1.96 us

profile of v3, /device:TPU:1, one launch (start us, length us, event | category | flops | bytes accessed | tf_op | source)
XLA Modules:
  0.0 25.4 jit_solution(5863173957837860414)
XLA Ops:
  1.3 22.1 %interpolate_and_migrate.1 = (f32[16,1024]{1,0:T(8,128)S(1)}, f32[8,16,768]{2,1,0:T(8,128)S(1)}, f32[8,16,128]{2,1,0:T(8,128)S(1)}, f32[3,256,1024]{2,1,0:T(8,128)S(1)}) custom-call(s32[1]{0:T(128)S(6)} %copy.14.live, s32[1,8]{1,0:T(1,128)} %counts.1, s32[1,8,16]{2,1,0:T(8,128)} %slots.1, s32[3,1024]{1,0:T(4,128)} %cell.1, s32[3,1024]{1,0:T(4,128)} %shift.1, ...), custom_call_target="tpu_custom_call" | custom-call | tf_op jit(solution)/shard_map/interpolate_and_migrate/pallas_call | solution.py:366
  23.4 2.0 %write_results.1 = (f32[3,1024]{1,0:T(4,128)}, f32[3,1024]{1,0:T(4,128)}, f32[3,256,1024]{2,1,0:T(8,128)}, f32[6,8,16]{2,1,0:T(8,128)}, f32[8,3,16,256]{3,2,1,0:T(8,128)}) custom-call(f32[16,1024]{1,0:T(8,128)S(1)} %get-tuple-element.14.res, f32[8,16,768]{2,1,0:T(8,128)S(1)} %get-tuple-element.15.rec_hist, f32[8,16,128]{2,1,0:T(8,128)S(1)} %get-tuple-element.16.rec_state, ...), custom_call_target="tpu_custom_call" | custom-call | tf_op jit(solution)/shard_map/write_results/pallas_call | solution.py:413
